TPU v7x, 256 devices: a whole 4x4x8 slice. The times are simulated.
256 devices in a mesh: bead: 32 (over z_hi, x, core), dom: 8 (over y, z_lo).
Axes of the slice: x: 4, y: 4, z: 8 (z_hi: 4, z_lo: 2; z = z_hi * 2 + z_lo), core: 2. Of those that a mesh axis runs over, the one named last changes fastest.
Arguments:
- positions: float32 [3, 32, 4096], P(None, 'bead', 'dom'), may hold values from -2.5 to 2.5
- momenta: float32 [3, 32, 4096], P(None, 'bead', 'dom'), may hold values from -6 to 6
- forces: float32 [3, 32, 4096], P(None, 'bead', 'dom'), may hold values from -6 to 6
- masses: float32 [4096], P('dom'), may hold values from 1 to 16
- charges: float32 [4096], P('dom'), may hold values from -1 to 1
- embedding: bfloat16 [4096, 240], P('dom'), may hold values from -6 to 6
- neighbours: int32 [8, 4096], P(None, 'dom'), may hold values from 0 to 895
- send_rows: int32 [3072], P('dom'), may hold values from 0 to 511
- wavevectors: int32 [3, 16384], replicated, may hold values from -12 to 12, as said below
- radial_weight: bfloat16 [2, 16, 240], replicated, may hold values from -1.5 to 1.5
- mix_weight: bfloat16 [2, 240, 240], replicated, may hold values from -0.375 to 0.375
- update_weight: bfloat16 [2, 240, 240], replicated, may hold values from -0.375 to 0.375
- readout_weight: bfloat16 [240, 240], replicated, may hold values from -0.375 to 0.375
- energy_weight: float32 [240], replicated, may hold values from -0.375 to 0.375
Outputs:
- next_positions: float32 [3, 32, 4096], P(None, 'bead', 'dom')
- next_momenta: float32 [3, 32, 4096], P(None, 'bead', 'dom')
- next_forces: float32 [3, 32, 4096], P(None, 'bead', 'dom')
Inputs may be any that keep to these rules, and one draw needn't show every extreme that they name: `wavevectors`: no component is zero.
All inputs are finite; a program needn't handle non-finite values.
Results may differ from a plain program's by a relative error of at most 0.0065.
Values may be sent and summed in bfloat16 or wider, within the bound.
A program may use at most 64 MiB of HBM per device.

v0:
```python
import math
import jax
import jax.numpy as jnp
from jax import lax
from jax.sharding import PartitionSpec as P

step_dt = 0.25
omega_cycle = 1.6
box_length = 4.0
ewald_sigma = 0.002
ewald_gain = 48.0
norm_eps = 1e-06
peak_frequency = lax.Precision.HIGHEST


def extended(cells, sides, width):
    for axis, dim in sides:
        count = lax.axis_size(axis)
        head = lax.slice_in_dim(cells, 0, width, axis=dim)
        tail = lax.slice_in_dim(cells, cells.shape[dim] - width, cells.shape[dim], axis=dim)
        cells = jnp.concatenate(
            [
                lax.ppermute(tail, axis, [(i, (i + 1) % count) for i in range(count)]),
                cells,
                lax.ppermute(head, axis, [((i + 1) % count, i) for i in range(count)]),
            ],
            axis=dim,
        )
    return cells


def mode_matrix(length):
    row_index = jnp.arange(length, dtype=jnp.int32)[:, None]
    column_index = jnp.arange(length, dtype=jnp.int32)[None, :]
    angles = 2.0 * math.pi / length * (row_index * column_index % length).astype(jnp.float32)
    single_norm = math.sqrt(1.0 / length)
    double_norm = math.sqrt(2.0 / length)
    parity = (1 - 2 * (row_index % 2)).astype(jnp.float32)
    middle = length // 2
    normal_transform = jnp.where(
        column_index == 0,
        single_norm,
        jnp.where(
            column_index < middle,
            double_norm * jnp.cos(angles),
            jnp.where(column_index == middle, single_norm * parity, double_norm * jnp.sin(angles)),
        ),
    )
    return normal_transform


def propagate(normal_mode_positions, normal_mode_momentum, masses):
    length = normal_mode_positions.shape[1]
    orders = jnp.arange(length, dtype=jnp.float32)
    omegas = 2.0 * omega_cycle * jnp.sin(math.pi * orders / length)
    cosine = jnp.cos(omegas * step_dt)[:, None]
    sines = jnp.sin(omegas * step_dt)
    omega_safe = jnp.where(orders == 0.0, 1.0, omegas)
    drift = jnp.where(orders == 0.0, step_dt, sines / omega_safe)[:, None]
    spring = (omegas * sines)[:, None]
    next_coords = cosine * normal_mode_positions + drift * normal_mode_momentum / masses
    next_moment = cosine * normal_mode_momentum - spring * masses * normal_mode_positions
    return (next_coords, next_moment)


def ewald_coef(reciprocal, atom_total):
    square = jnp.sum(reciprocal * reciprocal, 0)
    return (
        ewald_gain
        / math.sqrt(reciprocal.shape[1] * atom_total)
        * jnp.exp(-ewald_sigma * square)
        / square
    )


def phase_sums(reciprocal, centre, charge):
    phases = jnp.dot(reciprocal.T, centre, precision=peak_frequency)
    return (
        jnp.dot(jnp.cos(phases), charge, precision=peak_frequency),
        jnp.dot(jnp.sin(phases), charge, precision=peak_frequency),
    )


def ewald_force(reciprocal, centre, charge, cosine_sum, sine_sum, damping):
    phases = jnp.dot(reciprocal.T, centre, precision=peak_frequency)
    weight = (damping * cosine_sum)[:, None] * jnp.sin(phases) - (damping * sine_sum)[
        :, None
    ] * jnp.cos(phases)
    return 2.0 * charge * jnp.dot(reciprocal, weight, precision=peak_frequency)


def long_range(reciprocal, centre, charge, damping):
    cosine_part, sine_part = phase_sums(reciprocal, centre, charge)
    cosine_sum, sine_sum = lax.psum((cosine_part, sine_part), ("bead", "dom"))
    return ewald_force(reciprocal, centre, charge, cosine_sum, sine_sum, damping)


def advance(normal_mode_entries, mass_share, charge_share, reciprocal, damping):
    normal_mode_positions, normal_mode_momentum = propagate(
        normal_mode_entries[:3], normal_mode_entries[3:], mass_share
    )
    centre = normal_mode_positions[:, 0, :] / math.sqrt(normal_mode_entries.shape[1])
    long_force = long_range(reciprocal, centre, charge_share, damping)
    return (jnp.concatenate([normal_mode_positions, normal_mode_momentum], 0), long_force)


def layer_apply(
    hidden_own,
    extended_rows,
    extended_coords,
    neighbour_table,
    radial,
    mixing,
    update,
    radial_rates,
):
    owned_count = hidden_own.shape[0]
    owners = extended_coords[:, :owned_count]
    others = extended_coords[:, neighbour_table]
    offset = others - owners[:, None, :]
    distance = jnp.sum(offset * offset, 0)
    basis = (1.0 / (1.0 + radial_rates[:, None, None] * distance[None])).astype(jnp.bfloat16)
    edge_weight = jnp.einsum("mka,mf->kaf", basis, radial, preferred_element_type=jnp.float32)
    message = jnp.sum(edge_weight * extended_rows[neighbour_table], 0)
    scaled = message * lax.rsqrt(jnp.mean(message * message, -1, keepdims=True) + norm_eps)
    gated = jax.nn.silu(
        jnp.dot(scaled.astype(jnp.bfloat16), mixing, preferred_element_type=jnp.float32)
    ).astype(jnp.bfloat16)
    return hidden_own + jnp.dot(gated, update, preferred_element_type=jnp.float32)


def readout(hidden, readout_weight, energy_weight):
    activation = jax.nn.silu(
        jnp.dot(hidden.astype(jnp.bfloat16), readout_weight, preferred_element_type=jnp.float32)
    )
    return jnp.sum(activation * energy_weight)


def short_forces(
    coords,
    embedding,
    neighbours,
    send_rows,
    radial_weight,
    mix_weight,
    update_weight,
    readout_weight,
    energy_weight,
):
    owned_rows = coords.shape[2]
    ghost_rows = send_rows.shape[0] // 2
    to_before = send_rows[:ghost_rows]
    to_after = send_rows[ghost_rows:]
    radial_rates = 0.125 * 2.0 ** (0.5 * jnp.arange(radial_weight.shape[1], dtype=jnp.float32))
    apply_layer = jax.vmap(layer_apply, in_axes=(0, 0, 0, None, None, None, None, None))
    beside_all = extended(coords[:, :, send_rows], (("dom", 2),), ghost_rows)
    extended_coords = jnp.concatenate(
        [coords, beside_all[:, :, :ghost_rows], beside_all[:, :, 3 * ghost_rows :]], 2
    )
    extended_coords = jnp.moveaxis(extended_coords, 1, 0)
    hidden = embedding.astype(jnp.float32)[None]
    stored = []
    for number in range(mix_weight.shape[0]):
        rounded = hidden.astype(jnp.bfloat16)
        arrived = extended(rounded[:, send_rows, :], (("dom", 1),), ghost_rows)
        extended_rows = jnp.concatenate(
            [rounded, arrived[:, :ghost_rows], arrived[:, 3 * ghost_rows :]], 1
        ).astype(jnp.float32)
        stored.append((hidden, extended_rows))
        hidden = apply_layer(
            hidden,
            extended_rows,
            extended_coords,
            neighbours,
            radial_weight[number],
            mix_weight[number],
            update_weight[number],
            radial_rates,
        )
    cotan = jax.vmap(jax.grad(readout), in_axes=(0, None, None))(
        hidden, readout_weight, energy_weight
    )
    position_grad = jnp.zeros_like(extended_coords)
    for number in reversed(range(mix_weight.shape[0])):
        layer_input, extended_rows = stored[number]

        def local_layer(hidden_part, rows_part, coords_part):
            return apply_layer(
                hidden_part,
                rows_part,
                coords_part,
                neighbours,
                radial_weight[number],
                mix_weight[number],
                update_weight[number],
                radial_rates,
            )

        unused, pullback = jax.vjp(local_layer, layer_input, extended_rows, extended_coords)
        input_grad, feature_grad, position_part = pullback(cotan)
        position_grad = position_grad + position_part
        if number > 0:
            returned = extended(
                feature_grad[:, owned_rows:, :].astype(jnp.bfloat16), (("dom", 1),), ghost_rows
            ).astype(jnp.float32)
            owned_grad = (
                feature_grad[:, :owned_rows, :]
                .at[:, to_before, :]
                .add(returned[:, :ghost_rows])
                .at[:, to_after, :]
                .add(returned[:, 3 * ghost_rows :])
            )
            cotan = input_grad + owned_grad.astype(jnp.bfloat16).astype(jnp.float32)
    returned = extended(position_grad[:, :, owned_rows:], (("dom", 2),), ghost_rows)
    owned_force = (
        position_grad[:, :, :owned_rows]
        .at[:, :, to_before]
        .add(returned[:, :, :ghost_rows])
        .at[:, :, to_after]
        .add(returned[:, :, 3 * ghost_rows :])
    )
    return -jnp.moveaxis(owned_force, 0, 1)


def local(
    positions,
    momenta,
    forces,
    masses,
    charges,
    embedding,
    neighbours,
    send_rows,
    wavevectors,
    radial_weight,
    mix_weight,
    update_weight,
    readout_weight,
    energy_weight,
):
    beads_here = positions.shape[1]
    atom_count = positions.shape[2]
    bead_devices = lax.axis_size("bead")
    bead_slot = lax.axis_index("bead")
    bead_count = beads_here * bead_devices
    atom_share = atom_count // bead_devices
    normal_transform = mode_matrix(bead_count)
    bead_rows = lax.dynamic_slice_in_dim(normal_transform, bead_slot * beads_here, beads_here, 0)
    mass_share = lax.dynamic_slice_in_dim(masses, bead_slot * atom_share, atom_share, 0)
    charge_share = lax.dynamic_slice_in_dim(charges, bead_slot * atom_share, atom_share, 0)
    reciprocal = wavevectors.astype(jnp.float32) * (2.0 * math.pi / box_length)
    damping = ewald_coef(reciprocal, atom_count * lax.axis_size("dom"))
    coords_now, moment_now, force_now = (positions, momenta, forces)
    kicked = moment_now + 0.5 * step_dt * force_now
    stacked_arrays = jnp.concatenate([coords_now, kicked], 0)
    segment = stacked_arrays
    summed = lax.psum_scatter(
        jnp.einsum("bk,cba->ack", bead_rows, segment, precision=peak_frequency),
        "bead",
        scatter_dimension=0,
        tiled=True,
    )
    normal_mode_entries = jnp.transpose(summed, (1, 2, 0))
    joined, long_force = advance(normal_mode_entries, mass_share, charge_share, reciprocal, damping)
    packed = jnp.concatenate(
        [jnp.transpose(joined, (2, 0, 1)).reshape(atom_share, 6 * bead_count), long_force.T], 1
    )
    segment = lax.all_gather(packed, "bead", axis=0, tiled=True)
    row_count = segment.shape[0]
    coords = segment[:, : 6 * bead_count].reshape(row_count, 6, bead_count)
    restored = jnp.einsum("bk,ack->cba", bead_rows, coords, precision=peak_frequency)
    spread = segment[:, 6 * bead_count :].T[:, None, :]
    arrived = jnp.concatenate([restored, spread], 0)
    coords_now = arrived[:3]
    short_force = short_forces(
        coords_now,
        embedding,
        neighbours,
        send_rows,
        radial_weight,
        mix_weight,
        update_weight,
        readout_weight,
        energy_weight,
    )
    force_now = short_force + arrived[6:]
    moment_now = arrived[3:6] + 0.5 * step_dt * force_now
    return (coords_now, moment_now, force_now)


def solution(mesh):
    placed = (
        P(None, "bead", "dom"),
        P(None, "bead", "dom"),
        P(None, "bead", "dom"),
        P("dom"),
        P("dom"),
        P("dom", None),
        P(None, "dom"),
        P("dom"),
        P(),
        P(),
        P(),
        P(),
        P(),
        P(),
    )
    return jax.shard_map(
        local,
        mesh=mesh,
        in_specs=placed,
        out_specs=(P(None, "bead", "dom"), P(None, "bead", "dom"), P(None, "bead", "dom")),
        check_vma=False,
    )
```

profile of v0, /device:TPU:2, one launch (start us, length us, event | category | flops | bytes accessed | tf_op | source)
XLA Modules:
  0.0 636.9 jit_solution(1569555388232173794)
XLA Ops:
  7.3 0.8 multiply_add_fusion
  10.3 2.0 multiply_bitcast_fusion
  12.5 2.1 gather_fusion.2
  14.6 4.4 collective-permute-start.3
  21.1 85.0 %reduce-scatter.2.cloned.1.call-done = f32[16,6,32]{2,1,0:T(8,128)} async-done(((f32[512,6,32]{2,1,0:T(8,128)}), f32[16,6,32]{2,1,0:T(8,128)}) %reduce-scatter.2.cloned.1.call-update) | async-done | bytes 12304 | tf_op jit(solution)/shard_map/reduce_scatter | solution.py:257
  106.0 0.8 copy.158
  107.1 8.0 %fusion.207 = (f32[16384,16]{0,1:T(8,128)S(1)}, f32[16384,16]{0,1:T(8,128)S(1)}) fusion(f32[3,16]{1,0:T(4,128)S(1)} %fusion.160, s32[3,16384]{1,0:T(4,128)S(1)} %copy-done.11), kind=kOutput, calls=%fused_computation.258 | convolution fusion | flops 9535488 | bytes 2293952 | tf_op jit(solution)/shard_map/dot_general | solution.py:77
  115.0 1.3 fusion.186
  116.3 1.3 fusion.188
  117.8 240.3 %all-reduce.5.cloned.1.call-done = (f32[16384]{0:T(1024)}, f32[16384]{0:T(1024)}) async-done(((f32[16384]{0:T(1024)}, f32[16384]{0:T(1024)}), (f32[16384]{0:T(1024)}, f32[16384]{0:T(1024)})) %all-reduce.5.cloned.1.call-update) | async-done | bytes 131088 | tf_op jit(solution)/shard_map/psum | solution.py:94
  358.1 0.9 fusion.168
  359.0 1.4 convolution_multiply_fusion
  360.6 41.0 %all_gather.3 = f32[512,195]{1,0:T(8,128)S(1)} all-gather(f32[16,195]{1,0:T(8,128)S(1)} %pad_maximum_fusion.5), channel_id=1, replica_groups=mesh['bead'=32,'dom'=8] {'bead'}, dimensions={0}, use_global_device_ids=true | all-gather | bytes 411840 | tf_op jit(solution)/shard_map/all_gather | solution.py:268
  402.3 1.1 gather_fusion
  403.5 1.9 collective-permute-start.1
  406.1 16.1 %gather_fusion.3 = f32[4096,240]{1,0:T(8,128)} fusion(f32[896,240]{1,0:T(8,128)S(1)} %fusion.95, s32[4096]{0:T(1024)S(1)} %broadcast_clamp_fusion), kind=kCustom, calls=%fused_computation.3 | custom fusion | bytes 7880704 | tf_op jit(solution)/shard_map/vmap()/gather | solution.py:124
  422.2 5.3 copy.144
  427.5 5.3 copy.134
  433.6 10.8 %gather_fusion.1 = f32[4096,3]{1,0:T(8,128)S(1)} fusion(f32[3,896]{0,1:T(8,128)S(1)} %get-tuple-element.32, s32[4096]{0:T(1024)S(1)} %broadcast_clamp_fusion), kind=kCustom, calls=%fused_computation.1 | custom fusion | bytes 114688 | tf_op jit(solution)/shard_map/jvp(vmap())/gather | solution.py:119
  445.1 2.9 multiply_reduce_fusion.1
  448.4 1.1 fusion.213
  449.7 2.1 gather_fusion.4
  452.0 4.0 collective-permute-start.5
  456.2 2.6 fusion.124
  458.8 0.9 collective-permute-done.5
  459.8 3.4 collective-permute-done.4
  463.2 1.0 fusion.98
  464.2 1.5 copy.137
  465.7 16.1 %gather_fusion.5 = f32[4096,240]{1,0:T(8,128)} fusion(f32[896,240]{1,0:T(8,128)S(1)} %copy.137, s32[4096]{0:T(1024)S(1)} %broadcast_clamp_fusion), kind=kCustom, calls=%fused_computation.5 | custom fusion | bytes 7880704 | tf_op jit(solution)/shard_map/vmap()/gather | solution.py:124
  481.7 5.3 copy.139
  487.0 4.4 multiply_reduce_fusion
  491.5 1.0 fusion.106
  492.5 2.6 fusion.13
  495.1 2.1 convolution_convert_fusion.4
  497.3 2.5 multiply_reduce_fusion.4
  499.8 1.2 add_add_fusion.1
  501.7 4.7 broadcast_multiply_fusion
  506.4 5.2 copy.154
  511.6 23.1 %scatter_custom_fusion.1 = f32[896,240]{1,0:T(8,128)S(1)} fusion(s32[4096]{0:T(1024)S(1)} %bitcast.302, f32[4096,240]{1,0:T(8,128)} %bitcast.291, f32[]{:T(128)} %constant.51.clone.1), kind=kCustom, calls=%fused_computation.103 | custom fusion | flops 983040 | bytes 860672 | tf_op jit(solution)/shard_map/transpose(jvp(vmap()))/scatter-add | solution.py:124
  534.8 0.9 copy-done.12
  536.4 1.2 collective-permute-start.7
  537.5 0.8 collective-permute-start.6
  538.4 5.3 copy.140
  543.7 3.1 fusion.59
  546.8 0.8 slice_bitcast_fusion
  547.6 0.9 slice.166
  548.6 3.9 scatter_custom_fusion.2
  552.5 3.5 scatter_custom_fusion.3
  555.9 1.2 copy.143
  557.1 2.5 multiply_reduce_fusion.3
  559.7 1.2 add_add_fusion
  560.9 2.8 fusion.38
  563.7 3.1 add_multiply_fusion
  566.8 1.9 reduce_sum.128
  569.1 0.9 reduce_sum.134
  569.9 1.0 negate_bitcast_fusion
  571.7 22.8 %scatter_fusion = f32[3,896]{0,1:T(8,128)S(1)} fusion(f32[3,896]{0,1:T(8,128)S(1)} %pad_bitcast_fusion.1, s32[4096]{0:T(1024)S(1)} %bitcast.303, f32[4096,3]{1,0:T(8,128)} %bitcast.288), kind=kCustom, calls=%fused_computation.6 | custom fusion | flops 12288 | bytes 163840 | tf_op jit(solution)/shard_map/transpose(jvp(vmap()))/scatter-add | solution.py:119
  594.6 21.9 %scatter_fusion.1 = f32[3,896]{0,1:T(8,128)} fusion(f32[3,896]{0,1:T(8,128)} %pad_bitcast_fusion, s32[4096]{0:T(1024)S(1)} %bitcast.304, f32[4096,3]{1,0:T(8,128)S(1)} %bitcast.287), kind=kCustom, calls=%fused_computation.10 | custom fusion | flops 12288 | bytes 163840 | tf_op jit(solution)/shard_map/transpose(jvp(vmap()))/scatter-add | solution.py:119
  616.4 1.1 add_bitcast_fusion
  617.6 1.5 collective-permute-start.8
  619.1 2.7 collective-permute-start.9
  621.8 2.6 collective-permute-done.8
  624.4 1.8 scatter_custom_fusion.5
  626.2 1.9 scatter_custom_fusion.6
  (134 shorter events, 13.1 us)
Async XLA Ops:
  7.2 485.4 %copy-start = (bf16[240,240]{1,0:T(8,128)(2,1)S(1)}, bf16[240,240]{1,0:T(8,128)(2,1)}, u32[]{:S(2)}) copy-start(bf16[240,240]{1,0:T(8,128)(2,1)} %param.26) | copy-start | bytes 345604
  7.2 5.2 copy-start.14
  7.2 5.3 copy-start.26
  7.2 12.7 %copy-start.21 = (s32[8,512]{1,0:T(8,128)S(1)}, s32[8,512]{1,0:T(8,128)}, u32[]{:S(2)}) copy-start(s32[8,512]{1,0:T(8,128)} %param.20) | copy-start | bytes 49156
  7.2 12.7 %copy-start.27 = (f32[512]{0:T(512)S(1)}, f32[512]{0:T(512)}, u32[]{:S(2)}) copy-start(f32[512]{0:T(512)} %param.18) | copy-start | bytes 6148
  7.2 13.6 %copy-start.11 = (s32[3,16384]{1,0:T(4,128)S(1)}, s32[3,16384]{1,0:T(4,128)}, u32[]{:S(2)}) copy-start(s32[3,16384]{1,0:T(4,128)} %param.22) | copy-start | bytes 589828
  7.2 98.8 %reduce-scatter.2.cloned.1.call-start = ((), (), s32[]{:S(2)}) async-start(), calls=%async_computation.1 | async-start | bytes 2162688 | tf_op jit(solution)/shard_map/reduce_scatter | solution.py:257
  12.3 345.8 %all-reduce.5.cloned.1.call-start = ((), (), s32[]{:S(2)}) async-start(), calls=%async_computation.2 | async-start | bytes 262144 | tf_op jit(solution)/shard_map/psum | solution.py:94
  14.6 391.4 %collective-permute-start.3 = (bf16[1,192,240]{2,1,0:T(8,128)(2,1)S(1)}, bf16[1,192,240]{2,1,0:T(8,128)(2,1)S(1)}, u32[]{:S(2)}, u32[]{:S(2)}) collective-permute-start(bf16[1,192,240]{2,1,0:T(8,128)(2,1)S(1)} %get-tuple-element.38), channel_id=1, source_target_pairs={{1,0},{2,1},{3,2},{4,3},{5,4},{6,5},{7,6},{0,7},{9,8},{10,9},{11,1... | collective-permute-start | bytes 276488 | tf_op jit(solution)/shard_map/ppermute | solution.py:25
  19.1 387.0 %collective-permute-start.2 = (bf16[1,192,240]{2,1,0:T(8,128)(2,1)S(1)}, bf16[1,192,240]{2,1,0:T(8,128)(2,1)S(1)}, u32[]{:S(2)}, u32[]{:S(2)}) collective-permute-start(bf16[1,192,240]{2,1,0:T(8,128)(2,1)S(1)} %get-tuple-element.37), channel_id=1, source_target_pairs={{0,1},{1,2},{2,3},{3,4},{4,5},{5,6},{6,7},{7,0},{8,9},{9,10},{10,1... | collective-permute-start | bytes 276488 | tf_op jit(solution)/shard_map/ppermute | solution.py:23
  19.3 425.8 %copy-start.22 = (f32[16]{0:T(128)}, f32[16]{0:T(128)S(1)}, u32[]{:S(2)}) copy-start(f32[16]{0:T(128)S(1)} %power_multiply_fusion) | copy-start | bytes 196
  401.6 4.4 copy-start.6
  402.3 3.8 copy-start.9
  403.5 30.0 %collective-permute-start.1 = (f32[3,1,192]{0,2,1:T(8,128)S(1)}, f32[3,1,192]{0,2,1:T(8,128)S(1)}, u32[]{:S(2)}, u32[]{:S(2)}) collective-permute-start(f32[3,1,192]{0,2,1:T(8,128)S(1)} %get-tuple-element.36), channel_id=1, source_target_pairs={{1,0},{2,1},{3,2},{4,3},{5,4},{6,5},{7,6},{0,7},{9,8},{10,9},{11,1... | collective-permute-start | bytes 6920 | tf_op jit(solution)/shard_map/ppermute | solution.py:25
  405.4 28.1 %collective-permute-start = (f32[3,1,192]{0,2,1:T(8,128)S(1)}, f32[3,1,192]{0,2,1:T(8,128)S(1)}, u32[]{:S(2)}, u32[]{:S(2)}) collective-permute-start(f32[3,1,192]{0,2,1:T(8,128)S(1)} %get-tuple-element.35), channel_id=1, source_target_pairs={{0,1},{1,2},{2,3},{3,4},{4,5},{5,6},{6,7},{7,0},{8,9},{9,10},{10,1... | collective-permute-start | bytes 6920 | tf_op jit(solution)/shard_map/ppermute | solution.py:23
  432.8 12.3 %copy-start.18 = (bf16[2,16,240]{2,1,0:T(8,128)(2,1)S(1)}, bf16[2,16,240]{2,1,0:T(8,128)(2,1)}, u32[]{:S(2)}) copy-start(bf16[2,16,240]{2,1,0:T(8,128)(2,1)} %param.23) | copy-start | bytes 46084
  444.4 3.7 copy-start.16
  444.4 3.9 copy-start.15
  444.4 3.9 copy-start.28
  448.0 1.6 copy-start.2
  448.0 8.2 %copy-start.23 = (f32[16]{0:T(128)S(1)}, f32[16]{0:T(128)}, u32[]{:S(2)}) copy-start(f32[16]{0:T(128)} %copy-done.22) | copy-start | bytes 196
  448.1 10.8 %copy-start.19 = (f32[512]{0:T(512)}, f32[512]{0:T(512)S(1)}, u32[]{:S(2)}) copy-start(f32[512]{0:T(512)S(1)} %multiply_reduce_fusion.6) | copy-start | bytes 6148
  448.4 1.2 copy-start.13
  452.0 7.8 %collective-permute-start.5 = (bf16[1,192,240]{1,2,0:T(8,128)(2,1)S(1)}, bf16[1,192,240]{1,2,0:T(8,128)(2,1)S(1)}, u32[]{:S(2)}, u32[]{:S(2)}) collective-permute-start(bf16[1,192,240]{1,2,0:T(8,128)(2,1)S(1)} %get-tuple-element.40), channel_id=1, source_target_pairs={{1,0},{2,1},{3,2},{4,3},{5,4},{6,5},{7,6},{0,7},{9,8},{10,9},{11,1... | collective-permute-start | bytes 276488 | tf_op jit(solution)/shard_map/ppermute | solution.py:25
  456.1 7.1 %collective-permute-start.4 = (bf16[1,192,240]{1,2,0:T(8,128)(2,1)S(1)}, bf16[1,192,240]{1,2,0:T(8,128)(2,1)S(1)}, u32[]{:S(2)}, u32[]{:S(2)}) collective-permute-start(bf16[1,192,240]{1,2,0:T(8,128)(2,1)S(1)} %get-tuple-element.39), channel_id=1, source_target_pairs={{0,1},{1,2},{2,3},{3,4},{4,5},{5,6},{6,7},{7,0},{8,9},{9,10},{10,1... | collective-permute-start | bytes 276488 | tf_op jit(solution)/shard_map/ppermute | solution.py:23
  487.0 4.4 copy-start.17
  491.4 3.7 copy-start.29
  500.9 0.8 copy-start.8
  534.7 3.7 copy-start.4
  534.8 0.9 copy-start.12
  536.4 12.2 %collective-permute-start.7 = (bf16[1,192,240]{2,1,0:T(8,128)(2,1)}, bf16[1,192,240]{2,1,0:T(8,128)(2,1)S(1)}, u32[]{:S(2)}, u32[]{:S(2)}) collective-permute-start(bf16[1,192,240]{2,1,0:T(8,128)(2,1)} %get-tuple-element.30), channel_id=1, source_target_pairs={{1,0},{2,1},{3,2},{4,3},{5,4},{6,5},{7,6},{0,7},{9,8},{10,9},{11,1... | collective-permute-start | bytes 276488 | tf_op jit(solution)/shard_map/ppermute | solution.py:25
  537.5 11.1 %collective-permute-start.6 = (bf16[1,192,240]{2,1,0:T(8,128)(2,1)}, bf16[1,192,240]{2,1,0:T(8,128)(2,1)}, u32[]{:S(2)}, u32[]{:S(2)}) collective-permute-start(bf16[1,192,240]{2,1,0:T(8,128)(2,1)} %get-tuple-element.29), channel_id=1, source_target_pairs={{0,1},{1,2},{2,3},{3,4},{4,5},{5,6},{6,7},{7,0},{8,9},{9,10},{10,1... | collective-permute-start | bytes 276488 | tf_op jit(solution)/shard_map/ppermute | solution.py:23
  538.4 5.3 copy-start.24
  543.7 3.1 copy-start.5
  543.7 13.4 %copy-start.3 = (f32[512,240]{0,1:T(8,128)S(1)}, f32[512,240]{0,1:T(8,128)}, u32[]{:S(2)}) copy-start(f32[512,240]{0,1:T(8,128)} %copy-done.2) | copy-start | bytes 1474564
  546.8 12.9 %copy-start.20 = (f32[512]{0:T(512)S(1)}, f32[512]{0:T(512)}, u32[]{:S(2)}) copy-start(f32[512]{0:T(512)} %copy-done.19) | copy-start | bytes 6148
  548.6 12.2 %copy-start.25 = (f32[16]{0:T(128)S(1)}, f32[16]{0:T(128)}, u32[]{:S(2)}) copy-start(f32[16]{0:T(128)} %copy-done.22) | copy-start | bytes 196
  566.8 2.2 copy-start.1
  569.0 59.0 %copy-start.7 = (f32[512,195]{1,0:T(8,128)S(1)}, f32[512,195]{1,0:T(8,128)}, u32[]{:S(2)}) copy-start(f32[512,195]{1,0:T(8,128)} %copy-done.6) | copy-start | bytes 1198084
  569.0 59.0 %copy-start.10 = (f32[1,512,6]{2,1,0:T(8,128)S(1)}, f32[1,512,6]{2,1,0:T(8,128)}, u32[]{:S(2)}) copy-start(f32[1,512,6]{2,1,0:T(8,128)} %copy-done.9) | copy-start | bytes 36868
  617.6 6.8 %collective-permute-start.8 = (f32[1,3,192]{1,2,0:T(8,128)S(1)}, f32[1,3,192]{1,2,0:T(8,128)S(1)}, u32[]{:S(2)}, u32[]{:S(2)}) collective-permute-start(f32[1,3,192]{1,2,0:T(8,128)S(1)} %get-tuple-element.28), channel_id=1, source_target_pairs={{0,1},{1,2},{2,3},{3,4},{4,5},{5,6},{6,7},{7,0},{8,9},{9,10},{10,1... | collective-permute-start | bytes 6920 | tf_op jit(solution)/shard_map/ppermute | solution.py:23
  619.1 7.2 %collective-permute-start.9 = (f32[1,3,192]{1,2,0:T(8,128)S(1)}, f32[1,3,192]{1,2,0:T(8,128)S(1)}, u32[]{:S(2)}, u32[]{:S(2)}) collective-permute-start(f32[1,3,192]{1,2,0:T(8,128)S(1)} %get-tuple-element.27), channel_id=1, source_target_pairs={{1,0},{2,1},{3,2},{4,3},{5,4},{6,5},{7,6},{0,7},{9,8},{10,9},{11,1... | collective-permute-start | bytes 6920 | tf_op jit(solution)/shard_map/ppermute | solution.py:25
Sparse Core Ops, SparseCore 0:
  12.4 93.5 reduce-scatter.1
  117.8 240.2 all-reduce.4
where the time goes:
time: 645 us; the launch traced here: 637 us
  waiting for transfers between devices  332 us (51%)
  other arithmetic  107 us (17%)
  local copies, waits for them, and re-layouts  88.1 us (14%)
  blocking collectives  41 us (6%)
  matrix products  35.9 us (6%)
  starting transfers between devices  17.5 us (3%)
  between operations  15 us (2%)
    psum x1, waiting for transfers between devices, long_range(): cosine_sum, sine_sum = lax.psum((cosine_part, sine_part), ('bead', 'dom'))  240 us
    reduce_scatter x1, waiting for transfers between devices, local(): lax.psum_scatter(jnp.einsum('bk,cba->ack', bead_rows, segment, precision=...  85 us
    gather x6, local copies, waits for them, and re-layouts, layer_apply(): message = jnp.sum(edge_weight * extended_rows[neighbour_table], 0)  53.4 us
    scatter-add x2, other arithmetic, layer_apply(): others = extended_coords[:, neighbour_table]  44.7 us
    all_gather x1, blocking collectives, local(): segment = lax.all_gather(packed, 'bead', axis=0, tiled=True)  41 us
    scatter-add x1, other arithmetic, layer_apply(): message = jnp.sum(edge_weight * extended_rows[neighbour_table], 0)  23.1 us
    ppermute x5, starting transfers between devices, extended(): lax.ppermute(head, axis, [((i + 1) % count, i) for i in range(count)])  14.3 us
  transfers between devices with their start and end apart: 12, of which 5 were waited for; matrix products, arithmetic and copies ran while one was open for 10% of the time, Pallas kernels for 0%

commit v1 on v0

--- a/solution.py
+++ b/solution.py
@@ -11,6 +11,7 @@
 ewald_gain = 48.0
 norm_eps = 1e-06
 peak_frequency = lax.Precision.HIGHEST
+recover_rows = lambda u_in: lax.psum(lax.psum(u_in, axis_name="dom"), axis_name="bead")
 
 
 def extended(cells, sides, width):
@@ -91,7 +92,7 @@
 
 def long_range(reciprocal, centre, charge, damping):
     cosine_part, sine_part = phase_sums(reciprocal, centre, charge)
-    cosine_sum, sine_sum = lax.psum((cosine_part, sine_part), ("bead", "dom"))
+    cosine_sum, sine_sum = recover_rows((cosine_part, sine_part))
     return ewald_force(reciprocal, centre, charge, cosine_sum, sine_sum, damping)
 
 

time: 645 us -> 747 us (1.16)
  waiting for transfers between devices: 332 us -> 429 us
    psum x1 -> x2, waiting for transfers between devices: 240 us -> 337 us  [the longest x1 260 us: lax.psum(lax.psum(u_in, axis_name='dom'), axis_name='bead')]
  transfers between devices with their start and end apart: 12 -> 13, of which waited for: 5 -> 6; matrix products, arithmetic and copies ran while one was open for 10% -> 8% of each run, Pallas kernels for 0% -> 0%
where the time goes in v1:
time: 747 us; the launch traced here: 739 us
  waiting for transfers between devices  429 us (57%)
  other arithmetic  107 us (14%)
  local copies, waits for them, and re-layouts  88.4 us (12%)
  blocking collectives  45.2 us (6%)
  matrix products  36 us (5%)
  starting transfers between devices  19.1 us (3%)
  between operations  14.7 us (2%)
    psum x1, waiting for transfers between devices, lax.psum(lax.psum(u_in, axis_name='dom'), axis_name='bead')  260 us
    reduce_scatter x1, waiting for transfers between devices, local(): lax.psum_scatter(jnp.einsum('bk,cba->ack', bead_rows, segment, precision=...  85.2 us
    psum x1, waiting for transfers between devices, lax.psum(u_in, axis_name='dom')  76.3 us
    gather x6, local copies, waits for them, and re-layouts, layer_apply(): message = jnp.sum(edge_weight * extended_rows[neighbour_table], 0)  53.6 us
    all_gather x1, blocking collectives, local(): segment = lax.all_gather(packed, 'bead', axis=0, tiled=True)  45.2 us
    scatter-add x2, other arithmetic, layer_apply(): others = extended_coords[:, neighbour_table]  44.7 us
    scatter-add x1, other arithmetic, layer_apply(): message = jnp.sum(edge_weight * extended_rows[neighbour_table], 0)  23.1 us
    ppermute x5, starting transfers between devices, extended(): lax.ppermute(head, axis, [((i + 1) % count, i) for i in range(count)])  16 us
  transfers between devices with their start and end apart: 13, of which 6 were waited for; matrix products, arithmetic and copies ran while one was open for 8% of the time, Pallas kernels for 0%

profile of v1, /device:TPU:2, one launch (start us, length us, event | category | flops | bytes accessed | tf_op | source)
XLA Modules:
  0.0 739.3 jit_solution(15376381902577727895)
XLA Ops:
  10.3 2.0 multiply_bitcast_fusion
  12.5 2.1 gather_fusion.2
  14.6 4.4 collective-permute-start.3
  20.8 85.2 %reduce-scatter.2.cloned.1.call-done = f32[16,6,32]{2,1,0:T(8,128)} async-done(((f32[512,6,32]{2,1,0:T(8,128)}), f32[16,6,32]{2,1,0:T(8,128)}) %reduce-scatter.2.cloned.1.call-update) | async-done | bytes 12304 | tf_op jit(solution)/shard_map/reduce_scatter | solution.py:258
  106.0 0.8 copy.158
  107.0 8.0 %fusion.207 = (f32[16384,16]{0,1:T(8,128)S(1)}, f32[16384,16]{0,1:T(8,128)S(1)}) fusion(f32[3,16]{1,0:T(4,128)S(1)} %fusion.160, s32[3,16384]{1,0:T(4,128)S(1)} %copy-done.11), kind=kOutput, calls=%fused_computation.258 | convolution fusion | flops 9535488 | bytes 2293952 | tf_op jit(solution)/shard_map/dot_general | solution.py:78
  115.0 1.3 fusion.186
  116.3 1.3 fusion.188
  117.9 76.3 %all-reduce.9.cloned.1.call-done = (f32[16384]{0:T(1024)}, f32[16384]{0:T(1024)}) async-done(((f32[16384]{0:T(1024)}, f32[16384]{0:T(1024)}), (f32[16384]{0:T(1024)}, f32[16384]{0:T(1024)})) %all-reduce.9.cloned.1.call-update) | async-done | bytes 131088 | tf_op jit(solution)/shard_map/psum | solution.py:14
  194.4 260.2 %all-reduce.7.cloned.1.call-done = (f32[16384]{0:T(1024)}, f32[16384]{0:T(1024)}) async-done(((f32[16384]{0:T(1024)}, f32[16384]{0:T(1024)}), (f32[16384]{0:T(1024)}, f32[16384]{0:T(1024)})) %all-reduce.7.cloned.1.call-update) | async-done | bytes 131088 | tf_op jit(solution)/shard_map/psum | solution.py:14
  454.6 0.9 fusion.168
  455.5 1.4 convolution_multiply_fusion
  457.1 45.2 %all_gather.3 = f32[512,195]{1,0:T(8,128)S(1)} all-gather(f32[16,195]{1,0:T(8,128)S(1)} %pad_maximum_fusion.5), channel_id=1, replica_groups=mesh['bead'=32,'dom'=8] {'bead'}, dimensions={0}, use_global_device_ids=true | all-gather | bytes 411840 | tf_op jit(solution)/shard_map/all_gather | solution.py:269
  503.0 1.1 gather_fusion
  504.2 3.5 collective-permute-start.1
  508.2 16.2 %gather_fusion.3 = f32[4096,240]{1,0:T(8,128)} fusion(f32[896,240]{1,0:T(8,128)S(1)} %fusion.95, s32[4096]{0:T(1024)S(1)} %broadcast_clamp_fusion), kind=kCustom, calls=%fused_computation.3 | custom fusion | bytes 7880704 | tf_op jit(solution)/shard_map/vmap()/gather | solution.py:125
  524.4 5.3 copy.144
  529.7 5.3 copy.134
  535.8 10.8 %gather_fusion.1 = f32[4096,3]{1,0:T(8,128)S(1)} fusion(f32[3,896]{0,1:T(8,128)S(1)} %get-tuple-element.34, s32[4096]{0:T(1024)S(1)} %broadcast_clamp_fusion), kind=kCustom, calls=%fused_computation.1 | custom fusion | bytes 114688 | tf_op jit(solution)/shard_map/jvp(vmap())/gather | solution.py:120
  547.3 2.9 multiply_reduce_fusion.1
  550.6 1.1 fusion.213
  551.9 2.1 gather_fusion.4
  554.2 4.2 collective-permute-start.5
  558.6 2.6 fusion.124
  561.2 0.9 collective-permute-done.5
  562.1 3.4 collective-permute-done.4
  565.5 1.0 fusion.98
  566.5 1.5 copy.137
  568.0 16.2 %gather_fusion.5 = f32[4096,240]{1,0:T(8,128)} fusion(f32[896,240]{1,0:T(8,128)S(1)} %copy.137, s32[4096]{0:T(1024)S(1)} %broadcast_clamp_fusion), kind=kCustom, calls=%fused_computation.5 | custom fusion | bytes 7880704 | tf_op jit(solution)/shard_map/vmap()/gather | solution.py:125
  584.2 5.3 copy.139
  589.5 4.4 multiply_reduce_fusion
  593.9 1.1 fusion.106
  595.0 2.6 fusion.13
  597.6 2.1 convolution_convert_fusion.4
  599.7 2.5 multiply_reduce_fusion.4
  602.2 1.2 add_add_fusion.1
  604.2 4.7 broadcast_multiply_fusion
  608.9 5.2 copy.154
  614.1 23.1 %scatter_custom_fusion.1 = f32[896,240]{1,0:T(8,128)S(1)} fusion(s32[4096]{0:T(1024)S(1)} %bitcast.302, f32[4096,240]{1,0:T(8,128)} %bitcast.291, f32[]{:T(128)} %constant.51.clone.1), kind=kCustom, calls=%fused_computation.103 | custom fusion | flops 983040 | bytes 860672 | tf_op jit(solution)/shard_map/transpose(jvp(vmap()))/scatter-add | solution.py:125
  637.3 0.9 copy-done.12
  638.9 1.2 collective-permute-start.7
  640.1 0.8 collective-permute-start.6
  640.9 5.3 copy.140
  646.2 3.1 fusion.59
  649.3 0.8 slice_bitcast_fusion
  650.2 0.9 slice.166
  651.2 3.9 scatter_custom_fusion.2
  655.0 3.5 scatter_custom_fusion.3
  658.5 1.2 copy.143
  659.7 2.5 multiply_reduce_fusion.3
  662.2 1.2 add_add_fusion
  663.4 2.8 fusion.38
  666.2 3.2 add_multiply_fusion
  669.5 1.9 reduce_sum.128
  671.7 0.9 reduce_sum.134
  672.6 1.0 negate_bitcast_fusion
  674.3 22.8 %scatter_fusion = f32[3,896]{0,1:T(8,128)S(1)} fusion(f32[3,896]{0,1:T(8,128)S(1)} %pad_bitcast_fusion.1, s32[4096]{0:T(1024)S(1)} %bitcast.303, f32[4096,3]{1,0:T(8,128)} %bitcast.288), kind=kCustom, calls=%fused_computation.6 | custom fusion | flops 12288 | bytes 163840 | tf_op jit(solution)/shard_map/transpose(jvp(vmap()))/scatter-add | solution.py:120
  697.2 21.9 %scatter_fusion.1 = f32[3,896]{0,1:T(8,128)} fusion(f32[3,896]{0,1:T(8,128)} %pad_bitcast_fusion, s32[4096]{0:T(1024)S(1)} %bitcast.304, f32[4096,3]{1,0:T(8,128)S(1)} %bitcast.287), kind=kCustom, calls=%fused_computation.10 | custom fusion | flops 12288 | bytes 163840 | tf_op jit(solution)/shard_map/transpose(jvp(vmap()))/scatter-add | solution.py:120
  719.1 1.1 add_bitcast_fusion
  720.2 1.5 collective-permute-start.8
  721.7 2.7 collective-permute-start.9
  724.4 2.6 collective-permute-done.8
  727.0 1.8 scatter_custom_fusion.5
  728.9 1.9 scatter_custom_fusion.6
  (135 shorter events, 13.8 us)
Async XLA Ops:
  7.2 587.8 %copy-start = (bf16[240,240]{1,0:T(8,128)(2,1)S(1)}, bf16[240,240]{1,0:T(8,128)(2,1)}, u32[]{:S(2)}) copy-start(bf16[240,240]{1,0:T(8,128)(2,1)} %param.26) | copy-start | bytes 345604
  7.2 5.1 copy-start.14
  7.2 5.3 copy-start.25
  7.2 12.6 %copy-start.21 = (s32[8,512]{1,0:T(8,128)S(1)}, s32[8,512]{1,0:T(8,128)}, u32[]{:S(2)}) copy-start(s32[8,512]{1,0:T(8,128)} %param.20) | copy-start | bytes 49156
  7.2 12.6 %copy-start.26 = (f32[512]{0:T(512)S(1)}, f32[512]{0:T(512)}, u32[]{:S(2)}) copy-start(f32[512]{0:T(512)} %param.18) | copy-start | bytes 6148
  7.2 98.8 %reduce-scatter.2.cloned.1.call-start = ((), (), s32[]{:S(2)}) async-start(), calls=%async_computation.1 | async-start | bytes 2162688 | tf_op jit(solution)/shard_map/reduce_scatter | solution.py:258
  7.3 99.7 %copy-start.11 = (s32[3,16384]{1,0:T(4,128)S(1)}, s32[3,16384]{1,0:T(4,128)}, u32[]{:S(2)}) copy-start(s32[3,16384]{1,0:T(4,128)} %param.22) | copy-start | bytes 589828
  12.3 181.9 %all-reduce.9.cloned.1.call-start = ((), (), s32[]{:S(2)}) async-start(), calls=%async_computation.3 | async-start | bytes 262144 | tf_op jit(solution)/shard_map/psum | solution.py:14
  14.6 493.6 %collective-permute-start.3 = (bf16[1,192,240]{2,1,0:T(8,128)(2,1)S(1)}, bf16[1,192,240]{2,1,0:T(8,128)(2,1)S(1)}, u32[]{:S(2)}, u32[]{:S(2)}) collective-permute-start(bf16[1,192,240]{2,1,0:T(8,128)(2,1)S(1)} %get-tuple-element.40), channel_id=1, source_target_pairs={{1,0},{2,1},{3,2},{4,3},{5,4},{6,5},{7,6},{0,7},{9,8},{10,9},{11,1... | collective-permute-start | bytes 276488 | tf_op jit(solution)/shard_map/ppermute | solution.py:26
  19.0 489.1 %collective-permute-start.2 = (bf16[1,192,240]{2,1,0:T(8,128)(2,1)S(1)}, bf16[1,192,240]{2,1,0:T(8,128)(2,1)S(1)}, u32[]{:S(2)}, u32[]{:S(2)}) collective-permute-start(bf16[1,192,240]{2,1,0:T(8,128)(2,1)S(1)} %get-tuple-element.39), channel_id=1, source_target_pairs={{0,1},{1,2},{2,3},{3,4},{4,5},{5,6},{6,7},{7,0},{8,9},{9,10},{10,1... | collective-permute-start | bytes 276488 | tf_op jit(solution)/shard_map/ppermute | solution.py:24
  117.6 337.0 %all-reduce.7.cloned.1.call-start = ((), (), s32[]{:S(2)}) async-start(), calls=%async_computation.2 | async-start | bytes 262144 | tf_op jit(solution)/shard_map/psum | solution.py:14
  194.2 364.3 %copy-start.22 = (f32[16]{0:T(128)}, f32[16]{0:T(128)S(1)}, u32[]{:S(2)}) copy-start(f32[16]{0:T(128)S(1)} %power_multiply_fusion) | copy-start | bytes 196
  502.3 5.9 copy-start.6
  503.0 5.2 copy-start.9
  504.2 31.6 %collective-permute-start.1 = (f32[3,1,192]{0,2,1:T(8,128)S(1)}, f32[3,1,192]{0,2,1:T(8,128)S(1)}, u32[]{:S(2)}, u32[]{:S(2)}) collective-permute-start(f32[3,1,192]{0,2,1:T(8,128)S(1)} %get-tuple-element.38), channel_id=1, source_target_pairs={{1,0},{2,1},{3,2},{4,3},{5,4},{6,5},{7,6},{0,7},{9,8},{10,9},{11,1... | collective-permute-start | bytes 6920 | tf_op jit(solution)/shard_map/ppermute | solution.py:26
  507.7 28.1 %collective-permute-start = (f32[3,1,192]{0,2,1:T(8,128)S(1)}, f32[3,1,192]{0,2,1:T(8,128)S(1)}, u32[]{:S(2)}, u32[]{:S(2)}) collective-permute-start(f32[3,1,192]{0,2,1:T(8,128)S(1)} %get-tuple-element.37), channel_id=1, source_target_pairs={{0,1},{1,2},{2,3},{3,4},{4,5},{5,6},{6,7},{7,0},{8,9},{9,10},{10,1... | collective-permute-start | bytes 6920 | tf_op jit(solution)/shard_map/ppermute | solution.py:24
  535.0 12.3 %copy-start.18 = (bf16[2,16,240]{2,1,0:T(8,128)(2,1)S(1)}, bf16[2,16,240]{2,1,0:T(8,128)(2,1)}, u32[]{:S(2)}) copy-start(bf16[2,16,240]{2,1,0:T(8,128)(2,1)} %param.23) | copy-start | bytes 46084
  546.6 3.7 copy-start.16
  546.6 3.9 copy-start.15
  546.7 3.9 copy-start.27
  550.2 1.5 copy-start.2
  550.3 10.9 %copy-start.19 = (f32[512]{0:T(512)}, f32[512]{0:T(512)S(1)}, u32[]{:S(2)}) copy-start(f32[512]{0:T(512)S(1)} %multiply_reduce_fusion.6) | copy-start | bytes 6148
  550.6 1.2 copy-start.13
  554.2 7.9 %collective-permute-start.5 = (bf16[1,192,240]{1,2,0:T(8,128)(2,1)S(1)}, bf16[1,192,240]{1,2,0:T(8,128)(2,1)S(1)}, u32[]{:S(2)}, u32[]{:S(2)}) collective-permute-start(bf16[1,192,240]{1,2,0:T(8,128)(2,1)S(1)} %get-tuple-element.42), channel_id=1, source_target_pairs={{1,0},{2,1},{3,2},{4,3},{5,4},{6,5},{7,6},{0,7},{9,8},{10,9},{11,1... | collective-permute-start | bytes 276488 | tf_op jit(solution)/shard_map/ppermute | solution.py:26
  558.4 7.1 collective-permute-start.4
  589.5 4.4 copy-start.17
  593.8 3.8 copy-start.28
  603.4 0.8 copy-start.8
  637.2 3.7 copy-start.4
  637.3 0.9 copy-start.12
  638.9 12.2 %collective-permute-start.7 = (bf16[1,192,240]{2,1,0:T(8,128)(2,1)}, bf16[1,192,240]{2,1,0:T(8,128)(2,1)S(1)}, u32[]{:S(2)}, u32[]{:S(2)}) collective-permute-start(bf16[1,192,240]{2,1,0:T(8,128)(2,1)} %get-tuple-element.32), channel_id=1, source_target_pairs={{1,0},{2,1},{3,2},{4,3},{5,4},{6,5},{7,6},{0,7},{9,8},{10,9},{11,1... | collective-permute-start | bytes 276488 | tf_op jit(solution)/shard_map/ppermute | solution.py:26
  640.1 11.1 %collective-permute-start.6 = (bf16[1,192,240]{2,1,0:T(8,128)(2,1)}, bf16[1,192,240]{2,1,0:T(8,128)(2,1)}, u32[]{:S(2)}, u32[]{:S(2)}) collective-permute-start(bf16[1,192,240]{2,1,0:T(8,128)(2,1)} %get-tuple-element.31), channel_id=1, source_target_pairs={{0,1},{1,2},{2,3},{3,4},{4,5},{5,6},{6,7},{7,0},{8,9},{9,10},{10,1... | collective-permute-start | bytes 276488 | tf_op jit(solution)/shard_map/ppermute | solution.py:24
  640.9 5.3 copy-start.23
  646.2 3.1 copy-start.5
  646.2 13.4 %copy-start.3 = (f32[512,240]{0,1:T(8,128)S(1)}, f32[512,240]{0,1:T(8,128)}, u32[]{:S(2)}) copy-start(f32[512,240]{0,1:T(8,128)} %copy-done.2) | copy-start | bytes 1474564
  649.3 12.9 %copy-start.20 = (f32[512]{0:T(512)S(1)}, f32[512]{0:T(512)}, u32[]{:S(2)}) copy-start(f32[512]{0:T(512)} %copy-done.19) | copy-start | bytes 6148
  651.1 12.3 %copy-start.24 = (f32[16]{0:T(128)S(1)}, f32[16]{0:T(128)}, u32[]{:S(2)}) copy-start(f32[16]{0:T(128)} %copy-done.22) | copy-start | bytes 196
  669.5 2.2 copy-start.1
  671.7 59.0 %copy-start.7 = (f32[512,195]{1,0:T(8,128)S(1)}, f32[512,195]{1,0:T(8,128)}, u32[]{:S(2)}) copy-start(f32[512,195]{1,0:T(8,128)} %copy-done.6) | copy-start | bytes 1198084
  671.7 59.1 %copy-start.10 = (f32[1,512,6]{2,1,0:T(8,128)S(1)}, f32[1,512,6]{2,1,0:T(8,128)}, u32[]{:S(2)}) copy-start(f32[1,512,6]{2,1,0:T(8,128)} %copy-done.9) | copy-start | bytes 36868
  720.2 6.8 collective-permute-start.8
  721.7 7.2 collective-permute-start.9
Sparse Core Ops, SparseCore 0:
  12.4 93.5 reduce-scatter.1
  117.8 76.3 all-reduce.8
  197.1 257.4 all-reduce.6
